TPU v7x, 32 devices: a whole 2x2x4 slice. The times are simulated.
32 devices in a mesh: group: 2 (over core), blk: 16 (over z, y, x).
Axes of the slice: x: 2, y: 2, z: 4, core: 2. Of those that a mesh axis runs over, the one named last changes fastest.
Arguments:
- picture_vectors: bfloat16 [4096, 1152], P(('group', 'blk')), may hold values from -1 to 1
- caption_vectors: bfloat16 [4096, 1152], P(('group', 'blk')), may hold values from -1 to 1
- inverse_heat_factor: float32 [1], replicated, may hold values from 0.5 to 2
- score_shift_term: float32 [1], replicated, may hold values from -3 to 1
Outputs:
- grad_images: float32 [4096, 1152], P(('group', 'blk'))
- grad_texts: float32 [4096, 1152], P(('group', 'blk'))
- row_loss: float32 [4096], P(('group', 'blk'))
All inputs are finite; a program needn't handle non-finite values.
Results may differ from a plain program's by a relative error of at most 0.015.
Values may be sent and summed in bfloat16 or wider, within the bound.
A program may use at most 64 MiB of HBM per device.

v0:
```python
import jax
import jax.numpy as jnp
from jax import lax
from jax.sharding import PartitionSpec as P

SPAN = 2


def passed_along(array, axis, by):
    length = lax.axis_size(axis)
    return lax.ppermute(array, axis, [(i, (i + by) % length) for i in range(length)])


def contract_rows(left, right):
    return lax.dot_general(
        left, right, (((1,), (1,)), ((), ())), preferred_element_type=jnp.float32
    )


def contract_first(left, right):
    return lax.dot_general(
        left, right, (((0,), (0,)), ((), ())), preferred_element_type=jnp.float32
    )


def tile_terms(picture_vectors, text_bundle, positives, step, score_multiplier, shift_value):
    scaled = score_multiplier * contract_rows(picture_vectors, text_bundle) + shift_value
    if step == 0:
        signs = jnp.where(positives, 1.0, -1.0).astype(jnp.float32)
    else:
        signs = -jnp.ones_like(scaled)
    objective_piece = jnp.sum(jax.nn.softplus(-signs * scaled), axis=1)
    slopes = (-signs * jax.nn.sigmoid(-signs * scaled) * score_multiplier).astype(jnp.bfloat16)
    return (objective_piece, slopes)


def shards(picture_vectors, caption_vectors, inverse_heat_factor, score_shift_term):
    group_width = lax.axis_size("group")
    group_index = lax.axis_index("group")
    row_count = picture_vectors.shape[0]
    bundle_rows = row_count * group_width
    score_multiplier = inverse_heat_factor[0]
    shift_value = score_shift_term[0]
    text_bundle = lax.all_gather(caption_vectors, "group", axis=0, tiled=True)
    positives = (
        jnp.arange(bundle_rows)[None, :] == group_index * row_count + jnp.arange(row_count)[:, None]
    )
    loss_sum = jnp.zeros((row_count,), jnp.float32)
    grad_image = jnp.zeros(picture_vectors.shape, jnp.float32)
    carried_state = jnp.zeros((bundle_rows, picture_vectors.shape[1]), jnp.float32)
    for step in range(SPAN):
        objective_piece, slopes = tile_terms(
            picture_vectors, text_bundle, positives, step, score_multiplier, shift_value
        )
        loss_sum = loss_sum + objective_piece
        grad_image = grad_image + jnp.dot(slopes, text_bundle, preferred_element_type=jnp.float32)
        partial_value = contract_first(slopes, picture_vectors)
        carried_state = carried_state + partial_value
        if step + 1 < SPAN:
            carried_state = passed_along(carried_state.astype(jnp.bfloat16), "blk", 1).astype(
                carried_state.dtype
            )
        if step + 1 < SPAN:
            text_bundle = passed_along(text_bundle, "blk", 1)
    returned = passed_along(carried_state.astype(jnp.bfloat16), "blk", -(SPAN - 1)).astype(
        carried_state.dtype
    )
    grad_text = lax.psum_scatter(
        returned.astype(jnp.bfloat16), "group", scatter_dimension=0, tiled=True
    ).astype(jnp.float32)
    row_loss = loss_sum / (SPAN * bundle_rows)
    return (grad_image, grad_text, row_loss)


def solution(mesh):
    placed = (P(("group", "blk"), None), P(("group", "blk"), None), P(), P())
    return jax.shard_map(
        shards,
        mesh=mesh,
        in_specs=placed,
        out_specs=(P(("group", "blk"), None), P(("group", "blk"), None), P(("group", "blk"))),
        check_vma=False,
    )
```

profile of v0, /device:TPU:3, one launch (start us, length us, event | category | flops | bytes accessed | tf_op | source)
XLA Modules:
  0.0 76.0 jit_solution(2804868204561485574)
XLA Ops:
  7.2 0.0 copy-start
  7.2 0.0 reduce-scatter.2.cloned.1.call-start
  7.2 2.9 %all_gather.3 = bf16[256,1152]{1,0:T(8,128)(2,1)S(1)} all-gather(bf16[128,1152]{1,0:T(8,128)(2,1)} %param.5), channel_id=1, replica_groups=mesh['group'=2,'blk'=16] {'group'}, dimensions={0}, use_global_device_ids=true | all-gather | bytes 884736 | tf_op jit(solution)/shard_map/all_gather | solution.py:44
  10.1 1.2 %collective-permute-start = (bf16[256,1152]{1,0:T(8,128)(2,1)S(1)}, bf16[256,1152]{1,0:T(8,128)(2,1)S(1)}, u32[]{:S(2)}, u32[]{:S(2)}) collective-permute-start(bf16[256,1152]{1,0:T(8,128)(2,1)S(1)} %all_gather.3), channel_id=1, source_target_pairs={{0,1},{1,2},{2,3},{3,4},{4,5},{5,6},{6,7},{7,8},{8,9},{9,10},{10,1... | collective-permute-start | bytes 1769480 | tf_op jit(solution)/shard_map/ppermute | solution.py:11
  12.6 0.0 copy-done
  12.6 0.5 fusion.3
  13.1 0.4 convolution_convert_fusion
  13.6 1.3 %collective-permute-start.1 = (bf16[256,1152]{1,0:T(8,128)(2,1)S(1)}, bf16[256,1152]{1,0:T(8,128)(2,1)S(1)}, u32[]{:S(2)}, u32[]{:S(2)}) collective-permute-start(bf16[256,1152]{1,0:T(8,128)(2,1)S(1)} %convolution_convert_fusion), channel_id=1, source_target_pairs={{0,1},{1,2},{2,3},{3,4},{4,5},{5,6},{6,7},{7,8},{8,9},{9,10},{10,1... | collective-permute-start | bytes 1769480 | tf_op jit(solution)/shard_map/ppermute | solution.py:11
  14.8 9.8 %collective-permute-done = bf16[256,1152]{1,0:T(8,128)(2,1)S(1)} collective-permute-done((bf16[256,1152]{1,0:T(8,128)(2,1)S(1)}, bf16[256,1152]{1,0:T(8,128)(2,1)S(1)}, u32[]{:S(2)}, u32[]{:S(2)}) %collective-permute-start) | collective-permute-done | bytes 589856 | tf_op jit(solution)/shard_map/ppermute | solution.py:11
  24.6 0.5 fusion.4
  25.1 12.2 %collective-permute-done.1 = bf16[256,1152]{1,0:T(8,128)(2,1)S(1)} collective-permute-done((bf16[256,1152]{1,0:T(8,128)(2,1)S(1)}, bf16[256,1152]{1,0:T(8,128)(2,1)S(1)}, u32[]{:S(2)}, u32[]{:S(2)}) %collective-permute-start.1) | collective-permute-done | bytes 589856 | tf_op jit(solution)/shard_map/ppermute | solution.py:11
  37.3 0.4 add_convert_fusion
  37.7 4.4 %collective-permute-start.2 = (bf16[256,1152]{1,0:T(8,128)(2,1)S(1)}, bf16[256,1152]{1,0:T(8,128)(2,1)S(1)}, u32[]{:S(2)}, u32[]{:S(2)}) collective-permute-start(bf16[256,1152]{1,0:T(8,128)(2,1)S(1)} %add_convert_fusion), channel_id=1, source_target_pairs={{0,15},{1,0},{2,1},{3,2},{4,3},{5,4},{6,5},{7,6},{8,7},{9,8},{10,9... | collective-permute-start | bytes 1769480 | tf_op jit(solution)/shard_map/ppermute | solution.py:11
  42.0 11.8 %collective-permute-done.2 = bf16[256,1152]{1,0:T(8,128)(2,1)S(1)} collective-permute-done((bf16[256,1152]{1,0:T(8,128)(2,1)S(1)}, bf16[256,1152]{1,0:T(8,128)(2,1)S(1)}, u32[]{:S(2)}, u32[]{:S(2)}) %collective-permute-start.2) | collective-permute-done | bytes 589856 | tf_op jit(solution)/shard_map/ppermute | solution.py:11
  53.8 0.0 copy-start.1
  53.8 0.8 %copy-done.1 = bf16[256,1152]{1,0:T(8,128)(2,1)} copy-done((bf16[256,1152]{1,0:T(8,128)(2,1)}, bf16[256,1152]{1,0:T(8,128)(2,1)S(1)}, u32[]{:S(2)}) %copy-start.1) | copy-done | bytes 589848
  54.6 0.0 reduce-scatter.2.cloned.1.call-update
  54.6 0.3 fusion.6
  54.9 0.5 add_multiply_fusion
  55.4 1.1 %convolution_add_fusion = f32[128,1152]{1,0:T(8,128)} fusion(f32[128,1152]{1,0:T(8,128)S(1)} %fusion.6, bf16[256,1152]{1,0:T(8,128)(2,1)S(1)} %collective-permute-done, f32[128,256]{1,0:T(8,128)S(1)} %get-tuple-element.6, f32[]{:T(128)} %bitcast.11), kind=kOutput, calls=%fused_computation.1 | convolution fusion | flops 75808768 | bytes 1900548 | tf_op jit(solution)/shard_map/dot_general | solution.py:56
  56.5 10.9 %reduce-scatter.2.cloned.1.call-done = bf16[128,1152]{1,0:T(8,128)(2,1)} async-done(((bf16[256,1152]{1,0:T(8,128)(2,1)}), bf16[128,1152]{1,0:T(8,128)(2,1)}) %reduce-scatter.2.cloned.1.call-update) | async-done | bytes 294928 | tf_op jit(solution)/shard_map/reduce_scatter | solution.py:68
  67.4 1.8 %convert_element_type.25 = f32[128,1152]{1,0:T(8,128)} convert(bf16[128,1152]{1,0:T(8,128)(2,1)} %reduce-scatter.2.cloned.1.call-done) | non-fusion elementwise | flops 147456 | bytes 884736 | tf_op jit(solution)/shard_map/convert_element_type | solution.py:70
  (1 shorter events, 0.0 us)
Async XLA Ops:
  7.2 5.5 %copy-start = (bf16[128,1152]{1,0:T(8,128)(2,1)S(1)}, bf16[128,1152]{1,0:T(8,128)(2,1)}, u32[]{:S(2)}) copy-start(bf16[128,1152]{1,0:T(8,128)(2,1)} %param.4) | copy-start | bytes 884740
  7.2 60.2 %reduce-scatter.2.cloned.1.call-start = ((), (), s32[]{:S(2)}) async-start(), calls=%async_computation.1 | async-start | bytes 884736 | tf_op jit(solution)/shard_map/reduce_scatter | solution.py:68
  10.1 14.5 %collective-permute-start = (bf16[256,1152]{1,0:T(8,128)(2,1)S(1)}, bf16[256,1152]{1,0:T(8,128)(2,1)S(1)}, u32[]{:S(2)}, u32[]{:S(2)}) collective-permute-start(bf16[256,1152]{1,0:T(8,128)(2,1)S(1)} %all_gather.3), channel_id=1, source_target_pairs={{0,1},{1,2},{2,3},{3,4},{4,5},{5,6},{6,7},{7,8},{8,9},{9,10},{10,1... | collective-permute-start | bytes 1769480 | tf_op jit(solution)/shard_map/ppermute | solution.py:11
  13.6 23.7 %collective-permute-start.1 = (bf16[256,1152]{1,0:T(8,128)(2,1)S(1)}, bf16[256,1152]{1,0:T(8,128)(2,1)S(1)}, u32[]{:S(2)}, u32[]{:S(2)}) collective-permute-start(bf16[256,1152]{1,0:T(8,128)(2,1)S(1)} %convolution_convert_fusion), channel_id=1, source_target_pairs={{0,1},{1,2},{2,3},{3,4},{4,5},{5,6},{6,7},{7,8},{8,9},{9,10},{10,1... | collective-permute-start | bytes 1769480 | tf_op jit(solution)/shard_map/ppermute | solution.py:11
  37.7 16.1 %collective-permute-start.2 = (bf16[256,1152]{1,0:T(8,128)(2,1)S(1)}, bf16[256,1152]{1,0:T(8,128)(2,1)S(1)}, u32[]{:S(2)}, u32[]{:S(2)}) collective-permute-start(bf16[256,1152]{1,0:T(8,128)(2,1)S(1)} %add_convert_fusion), channel_id=1, source_target_pairs={{0,15},{1,0},{2,1},{3,2},{4,3},{5,4},{6,5},{7,6},{8,7},{9,8},{10,9... | collective-permute-start | bytes 1769480 | tf_op jit(solution)/shard_map/ppermute | solution.py:11
  53.8 0.8 %copy-start.1 = (bf16[256,1152]{1,0:T(8,128)(2,1)}, bf16[256,1152]{1,0:T(8,128)(2,1)S(1)}, u32[]{:S(2)}) copy-start(bf16[256,1152]{1,0:T(8,128)(2,1)S(1)} %collective-permute-done.2) | copy-start | bytes 1769476
Sparse Core Ops, SparseCore 0:
  54.7 12.5 reduce-scatter.1
where the time goes:
time: 77 us; the launch traced here: 76 us
  waiting for transfers between devices  44.6 us (58%)
  between operations  15.4 us (20%)
  starting transfers between devices  6.88 us (9%)
  matrix products  3.12 us (4%)
  blocking collectives  2.87 us (4%)
  other arithmetic  2.33 us (3%)
  local copies, waits for them, and re-layouts  0.82 us (1%)
    ppermute x3, waiting for transfers between devices, passed_along(): lax.ppermute(array, axis, [(i, (i + by) % length) for i in range(length)])  33.7 us
    reduce_scatter x1, waiting for transfers between devices, shards(): lax.psum_scatter(returned.astype(jnp.bfloat16), 'group', scatter_dimensio...  10.9 us
    ppermute x3, starting transfers between devices, passed_along(): lax.ppermute(array, axis, [(i, (i + by) % length) for i in range(length)])  6.85 us
    all_gather x1, blocking collectives, shards(): text_bundle = lax.all_gather(caption_vectors, 'group', axis=0, tiled=True)  2.87 us
    convert_element_type x1, other arithmetic, shards(): grad_text = lax.psum_scatter(returned.astype(jnp.bfloat16), 'group', scat...  1.81 us
  transfers between devices with their start and end apart: 4, of which 4 were waited for; matrix products, arithmetic and copies ran while one was open for 4% of the time, Pallas kernels for 0%

commit v1 on v0

v1 whole, which is shorter than its diff:
```python
import functools

import jax
import jax.numpy as jnp
from jax import lax
from jax.experimental import pallas as pl
from jax.experimental.pallas import tpu as pltpu
from jax.sharding import PartitionSpec as P

SPAN = 2
PIECES = 4
TEXT, IMAGE = 0, 1


def kernel(
    group_width, cycle, images, texts, scale, shift, grad_images, grad_texts, row_loss,
    near, far, load_sem, near_send, near_recv, far_send, far_recv, pass_send, pass_recv,
):
    group, place = lax.axis_index("group"), lax.axis_index("blk")
    after, before = lax.rem(place + 1, cycle), lax.rem(place + cycle - 1, cycle)
    rows = images.shape[0]
    piece = rows // PIECES
    sources = (texts, images)
    onward = (after, before)

    def peer(k):
        return lax.rem(group + k, group_width)

    def over_peers(body):
        if group_width <= 2:
            for k in range(1, group_width):
                body(k)
        else:
            pl.loop(1, group_width)(body)

    def loads(kind):
        return pltpu.make_async_copy(sources[kind], near.at[kind, group], load_sem.at[kind])

    def near_copy(kind, k):
        return pltpu.make_async_remote_copy(
            src_ref=sources[kind], dst_ref=near.at[kind, group],
            send_sem=near_send.at[kind, k], recv_sem=near_recv.at[kind, k],
            device_id=(peer(k), place), device_id_type=pl.DeviceIdType.MESH,
        )

    def far_copy(kind, c):
        part = pl.ds(c * piece, piece)
        return pltpu.make_async_remote_copy(
            src_ref=sources[kind].at[part], dst_ref=far.at[kind, group, part],
            send_sem=far_send.at[kind, c], recv_sem=far_recv.at[kind, c],
            device_id=(group, onward[kind]), device_id_type=pl.DeviceIdType.MESH,
        )

    def pass_copy(kind, c, k):
        block = far.at[kind, group, pl.ds(c * piece, piece)]
        return pltpu.make_async_remote_copy(
            src_ref=block, dst_ref=block,
            send_sem=pass_send.at[kind, c, k], recv_sem=pass_recv.at[kind, c, k],
            device_id=(peer(k), place), device_id_type=pl.DeviceIdType.MESH,
        )

    def sender(k):
        return lax.rem(group + group_width - k, group_width)

    for kind in (TEXT, IMAGE):
        loads(kind).start()
    barrier = pltpu.get_barrier_semaphore()
    for neighbour in (after, before):
        pl.semaphore_signal(
            barrier, inc=1, device_id=(group, neighbour), device_id_type=pl.DeviceIdType.MESH
        )

    def greet(k):
        pl.semaphore_signal(
            barrier, inc=1, device_id=(peer(k), place), device_id_type=pl.DeviceIdType.MESH
        )

    over_peers(greet)
    pl.semaphore_wait(barrier, group_width + 1)

    for c in range(PIECES):
        for kind in (TEXT, IMAGE):
            far_copy(kind, c).start()
    for kind in (TEXT, IMAGE):
        over_peers(lambda k: near_copy(kind, k).start())

    factor, offset = scale[0], shift[0]
    outputs = (grad_images, grad_texts)

    def meet(kind, block, diagonal=False, first=False):
        own = near[1 - kind, group]
        z = lax.dot_general(
            block, own, (((1,), (1,)), ((), ())), preferred_element_type=jnp.float32
        )
        z = factor * z + offset
        if diagonal:
            same = lax.broadcasted_iota(jnp.int32, z.shape, 0) == lax.broadcasted_iota(
                jnp.int32, z.shape, 1
            )
            z = jnp.where(same, -z, z)
        small = jnp.exp(-jnp.abs(z))
        slopes = factor * (jnp.where(z >= 0, 1.0, small) / (1.0 + small))
        if diagonal:
            slopes = jnp.where(same, -slopes, slopes)
        if kind == TEXT:
            loss = jnp.sum(jnp.maximum(z, 0.0) + jnp.log1p(small), axis=0, keepdims=True)
            row_loss[...] = loss if first else row_loss[...] + loss
        grad = lax.dot_general(
            slopes.astype(jnp.bfloat16), block, (((0,), (0,)), ((), ())),
            preferred_element_type=jnp.float32,
        )
        out = outputs[kind]
        out[...] = grad if first else out[...] + grad

    for kind in (TEXT, IMAGE):
        loads(kind).wait()
    for kind in (TEXT, IMAGE):
        meet(kind, near[kind, group], diagonal=True, first=True)

    def meet_near(k):
        for kind in (TEXT, IMAGE):
            near_copy(kind, k).wait_recv()
            meet(kind, near[kind, sender(k)])

    over_peers(meet_near)

    def meet_passed(c):
        def one(k):
            for kind in (TEXT, IMAGE):
                pass_copy(kind, c, k).wait_recv()
                meet(kind, far[kind, sender(k), pl.ds(c * piece, piece)])

        over_peers(one)

    for c in range(PIECES):
        for kind in (TEXT, IMAGE):
            far_copy(kind, c).wait_recv()
            over_peers(lambda k: pass_copy(kind, c, k).start())
        if c > 0:
            meet_passed(c - 1)
        for kind in (TEXT, IMAGE):
            meet(kind, far[kind, group, pl.ds(c * piece, piece)])
    meet_passed(PIECES - 1)
    row_loss[...] = row_loss[...] / (SPAN * group_width * rows)

    for kind in (TEXT, IMAGE):
        for c in range(PIECES):
            far_copy(kind, c).wait_send()

    def sent(k):
        for kind in (TEXT, IMAGE):
            near_copy(kind, k).wait_send()
            for c in range(PIECES):
                pass_copy(kind, c, k).wait_send()

    over_peers(sent)


def shards(group_width, cycle, images, texts, scale, shift):
    rows, width = images.shape
    flops = 4 * 2 * rows * SPAN * group_width * rows * width
    grad_images, grad_texts, row_loss = pl.pallas_call(
        functools.partial(kernel, group_width, cycle),
        out_shape=(
            jax.ShapeDtypeStruct((rows, width), jnp.float32),
            jax.ShapeDtypeStruct((rows, width), jnp.float32),
            jax.ShapeDtypeStruct((1, rows), jnp.float32),
        ),
        in_specs=[pl.BlockSpec(memory_space=pl.ANY)] * 2
        + [pl.BlockSpec(memory_space=pltpu.SMEM)] * 2,
        out_specs=[pl.BlockSpec(memory_space=pltpu.VMEM)] * 3,
        scratch_shapes=[
            pltpu.VMEM((2, group_width, rows, width), images.dtype),
            pltpu.VMEM((2, group_width, rows, width), images.dtype),
            pltpu.SemaphoreType.DMA((2,)),
            pltpu.SemaphoreType.DMA((2, group_width)),
            pltpu.SemaphoreType.DMA((2, group_width)),
            pltpu.SemaphoreType.DMA((2, PIECES)),
            pltpu.SemaphoreType.DMA((2, PIECES)),
            pltpu.SemaphoreType.DMA((2, PIECES, group_width)),
            pltpu.SemaphoreType.DMA((2, PIECES, group_width)),
        ],
        compiler_params=pltpu.CompilerParams(
            collective_id=0, has_side_effects=True, vmem_limit_bytes=32 << 20
        ),
        cost_estimate=pl.CostEstimate(
            flops=flops, bytes_accessed=16 * rows * width, transcendentals=0
        ),
    )(images, texts, scale, shift)
    return grad_images, grad_texts, row_loss.reshape(rows)


def solution(mesh):
    placed = (P(("group", "blk"), None), P(("group", "blk"), None), P(), P())
    return jax.shard_map(
        functools.partial(shards, mesh.shape["group"], mesh.shape["blk"]),
        mesh=mesh,
        in_specs=placed,
        out_specs=(P(("group", "blk"), None), P(("group", "blk"), None), P(("group", "blk"))),
        check_vma=False,
    )
```

time: 77 us -> 27.5 us (0.36)
  waiting for transfers between devices: 44.6 us -> 0 us
  Pallas kernels: 0 us -> 21.3 us
  between operations: 15.4 us -> 1.94 us
  starting transfers between devices: 6.88 us -> 0 us
  local copies, waits for them, and re-layouts: 0.82 us -> 4.06 us
  matrix products: 3.12 us -> 0 us
  blocking collectives: 2.87 us -> 0 us
  other arithmetic: 2.33 us -> 0 us
    ppermute x3 -> x0, waiting for transfers between devices: 33.7 us -> none  [passed_along(): lax.ppermute(array, axis, [(i, (i + by) % length) for i in range(length)])]
    pallas_call x0 -> x1, Pallas kernels: none -> 21.3 us  [shards(): pl.pallas_call(functools.partial(kernel, group_width, cycle), out_shape=(...]
    reduce_scatter x1 -> x0, waiting for transfers between devices: 10.9 us -> none  [shards(): lax.psum_scatter(returned.astype(jnp.bfloat16), 'group', scatter_dimensio...]
    ppermute x3 -> x0, starting transfers between devices: 6.85 us -> none  [passed_along(): lax.ppermute(array, axis, [(i, (i + by) % length) for i in range(length)])]
    unnamed x4 -> x7, local copies, waits for them, and re-layouts: 0.82 us -> 4.06 us
    dot_general x6 -> x0, matrix products: 3.12 us -> none  [the longest x2 1.36 us: shards(): jnp.dot(slopes, text_bundle, preferred_element_type=jnp.float32)]
    all_gather x1 -> x0, blocking collectives: 2.87 us -> none  [shards(): text_bundle = lax.all_gather(caption_vectors, 'group', axis=0, tiled=True)]
    convert_element_type x1 -> x0, other arithmetic: 1.81 us -> none  [shards(): grad_text = lax.psum_scatter(returned.astype(jnp.bfloat16), 'group', scat...]
  transfers between devices with their start and end apart: 4 -> 0, of which waited for: 4 -> 0; matrix products, arithmetic and copies ran while one was open for 4% -> 0% of each run, Pallas kernels for 0% -> 0%
where the time goes in v1:
time: 27.5 us; the launch traced here: 27.3 us
  Pallas kernels  21.3 us (77%)
  local copies, waits for them, and re-layouts  4.06 us (15%)
  between operations  1.94 us (7%)
    pallas_call x1, Pallas kernels, shards(): pl.pallas_call(functools.partial(kernel, group_width, cycle), out_shape=(...  21.3 us
    unnamed x7, local copies, waits for them, and re-layouts  4.06 us

profile of v1, /device:TPU:3, one launch (start us, length us, event | category | flops | bytes accessed | tf_op | source)
XLA Modules:
  0.0 27.3 jit_solution(908741070797671499)
XLA Ops:
  1.9 0.0 copy-start
  1.9 1.0 %copy-done = bf16[128,1152]{1,0:T(8,128)(2,1)S(1)} copy-done((bf16[128,1152]{1,0:T(8,128)(2,1)S(1)}, bf16[128,1152]{1,0:T(8,128)(2,1)}, u32[]{:S(2)}) %copy-start) | copy-done | bytes 294936
  2.9 0.0 copy-start.1
  2.9 1.0 %copy-done.1 = bf16[128,1152]{1,0:T(8,128)(2,1)S(1)} copy-done((bf16[128,1152]{1,0:T(8,128)(2,1)S(1)}, bf16[128,1152]{1,0:T(8,128)(2,1)}, u32[]{:S(2)}) %copy-start.1) | copy-done | bytes 294936
  3.8 21.3 %shard_map.67 = (f32[128,1152]{1,0:T(8,128)S(1)}, f32[128,1152]{1,0:T(8,128)S(1)}, f32[1,128]{1,0:T(1,128)S(1)}) custom-call(bf16[128,1152]{1,0:T(8,128)(2,1)S(1)} %copy-done, bf16[128,1152]{1,0:T(8,128)(2,1)S(1)} %copy-done.1, f32[1]{0:T(128)S(6)} %copy.10.scale, f32[1]{0:T(128)S(6)} %copy.11.shift), custom_call_target="tpu_custom_call" | custom-call | flops 603979776 | bytes 2359296 | tf_op jit(solution)/shard_map/pallas_call | solution.py:162
  25.1 0.8 %copy.12 = f32[128,1152]{1,0:T(8,128)} copy(f32[128,1152]{1,0:T(8,128)S(1)} %get-tuple-element.12) | data formatting | bytes 1179648
  25.9 0.8 %copy.13 = f32[128,1152]{1,0:T(8,128)} copy(f32[128,1152]{1,0:T(8,128)S(1)} %get-tuple-element.13) | data formatting | bytes 1179648
  26.7 0.5 %copy.14 = f32[128]{0:T(128)} copy(f32[128]{0:T(128)S(1)} %bitcast.1) | data formatting | bytes 1024
Async XLA Ops:
  1.9 1.0 %copy-start = (bf16[128,1152]{1,0:T(8,128)(2,1)S(1)}, bf16[128,1152]{1,0:T(8,128)(2,1)}, u32[]{:S(2)}) copy-start(bf16[128,1152]{1,0:T(8,128)(2,1)} %images.1) | copy-start | bytes 884740
  2.9 1.0 %copy-start.1 = (bf16[128,1152]{1,0:T(8,128)(2,1)S(1)}, bf16[128,1152]{1,0:T(8,128)(2,1)}, u32[]{:S(2)}) copy-start(bf16[128,1152]{1,0:T(8,128)(2,1)} %texts.1) | copy-start | bytes 884740

commit v2 on v1

--- a/solution.py
+++ b/solution.py
@@ -156,17 +156,28 @@
     over_peers(sent)
 
 
+def store(*refs):
+    count = len(refs) // 2
+    held, out, sem = refs[:count], refs[count:-1], refs[-1]
+    copies = [pltpu.make_async_copy(a, b, sem.at[i]) for i, (a, b) in enumerate(zip(held, out))]
+    for copy in copies:
+        copy.start()
+    for copy in copies:
+        copy.wait()
+
+
 def shards(group_width, cycle, images, texts, scale, shift):
     rows, width = images.shape
     flops = 4 * 2 * rows * SPAN * group_width * rows * width
-    grad_images, grad_texts, row_loss = pl.pallas_call(
+    shapes = (
+        jax.ShapeDtypeStruct((rows, width), jnp.float32),
+        jax.ShapeDtypeStruct((rows, width), jnp.float32),
+        jax.ShapeDtypeStruct((1, rows), jnp.float32),
+    )
+    results = pl.pallas_call(
         functools.partial(kernel, group_width, cycle),
-        out_shape=(
-            jax.ShapeDtypeStruct((rows, width), jnp.float32),
-            jax.ShapeDtypeStruct((rows, width), jnp.float32),
-            jax.ShapeDtypeStruct((1, rows), jnp.float32),
-        ),
-        in_specs=[pl.BlockSpec(memory_space=pl.ANY)] * 2
+        out_shape=shapes,
+        in_specs=[pl.BlockSpec(memory_space=pltpu.HBM)] * 2
         + [pl.BlockSpec(memory_space=pltpu.SMEM)] * 2,
         out_specs=[pl.BlockSpec(memory_space=pltpu.VMEM)] * 3,
         scratch_shapes=[
@@ -186,7 +197,23 @@
         cost_estimate=pl.CostEstimate(
             flops=flops, bytes_accessed=16 * rows * width, transcendentals=0
         ),
-    )(images, texts, scale, shift)
+    )(
+        pltpu.with_memory_space_constraint(images, pltpu.HBM),
+        pltpu.with_memory_space_constraint(texts, pltpu.HBM),
+        scale,
+        shift,
+    )
+    grad_images, grad_texts, row_loss = pl.pallas_call(
+        store,
+        out_shape=shapes,
+        in_specs=[pl.BlockSpec(memory_space=pltpu.VMEM)] * 3,
+        out_specs=[pl.BlockSpec(memory_space=pltpu.HBM)] * 3,
+        scratch_shapes=[pltpu.SemaphoreType.DMA((3,))],
+        compiler_params=pltpu.CompilerParams(vmem_limit_bytes=8 << 20),
+        cost_estimate=pl.CostEstimate(
+            flops=0, bytes_accessed=16 * rows * width, transcendentals=0
+        ),
+    )(*results)
     return grad_images, grad_texts, row_loss.reshape(rows)
 
 

time: 27.5 us -> 24.6 us (0.89)
  local copies, waits for them, and re-layouts: 4.06 us -> 0 us
  Pallas kernels: 21.3 us -> 22.4 us
    unnamed x7 -> x0, local copies, waits for them, and re-layouts: 4.06 us -> none
    pallas_call x1 -> x2, Pallas kernels: 21.3 us -> 22.4 us  [the longest x1 21.4 us: shards(): pl.pallas_call(functools.partial(kernel, group_width, cycle), out_shape=s...]
where the time goes in v2:
time: 24.6 us; the launch traced here: 24.3 us
  Pallas kernels  22.4 us (91%)
  between operations  1.93 us (8%)
    pallas_call x1, Pallas kernels, shards(): pl.pallas_call(functools.partial(kernel, group_width, cycle), out_shape=s...  21.4 us
    pallas_call x1, Pallas kernels, shards(): pl.pallas_call(store, out_shape=shapes, in_specs=[pl.BlockSpec(memory_spa...  1.04 us

profile of v2, /device:TPU:3, one launch (start us, length us, event | category | flops | bytes accessed | tf_op | source)
XLA Modules:
  0.0 24.3 jit_solution(16205637969707352696)
XLA Ops:
  1.9 21.4 %shard_map.67 = (f32[128,1152]{1,0:T(8,128)S(1)}, f32[128,1152]{1,0:T(8,128)S(1)}, f32[1,128]{1,0:T(1,128)S(1)}) custom-call(bf16[128,1152]{1,0:T(8,128)(2,1)} %images.1, bf16[128,1152]{1,0:T(8,128)(2,1)} %texts.1, f32[1]{0:T(128)S(6)} %copy.7.scale, f32[1]{0:T(128)S(6)} %copy.8.shift), custom_call_target="tpu_custom_call" | custom-call | flops 603979776 | bytes 2359296 | tf_op jit(solution)/shard_map/pallas_call | solution.py:177
  23.3 1.0 %shard_map.68 = (f32[128,1152]{1,0:T(8,128)}, f32[128,1152]{1,0:T(8,128)}, f32[1,128]{1,0:T(1,128)}) custom-call(f32[128,1152]{1,0:T(8,128)S(1)} %get-tuple-element.9.refs_0_, f32[128,1152]{1,0:T(8,128)S(1)} %get-tuple-element.10.refs_1_, f32[1,128]{1,0:T(1,128)S(1)} %get-tuple-element.11.refs_2_), custom_call_target="tpu_custom_call" | custom-call | bytes 2359296 | tf_op jit(solution)/shard_map/pallas_call | solution.py:206

commit v3 on v2

--- a/solution.py
+++ b/solution.py
@@ -33,34 +33,35 @@
         else:
             pl.loop(1, group_width)(body)
 
+    def own(kind):
+        return near.at[kind, pl.ds(pl.multiple_of(group * rows, rows), rows)]
+
+    def own_piece(kind, c):
+        return far.at[kind, c, pl.ds(pl.multiple_of(group * piece, piece), piece)]
+
     def loads(kind):
-        return pltpu.make_async_copy(sources[kind], near.at[kind, group], load_sem.at[kind])
+        return pltpu.make_async_copy(sources[kind], own(kind), load_sem.at[kind])
 
     def near_copy(kind, k):
         return pltpu.make_async_remote_copy(
-            src_ref=sources[kind], dst_ref=near.at[kind, group],
+            src_ref=sources[kind], dst_ref=own(kind),
             send_sem=near_send.at[kind, k], recv_sem=near_recv.at[kind, k],
             device_id=(peer(k), place), device_id_type=pl.DeviceIdType.MESH,
         )
 
     def far_copy(kind, c):
-        part = pl.ds(c * piece, piece)
         return pltpu.make_async_remote_copy(
-            src_ref=sources[kind].at[part], dst_ref=far.at[kind, group, part],
+            src_ref=sources[kind].at[pl.ds(c * piece, piece)], dst_ref=own_piece(kind, c),
             send_sem=far_send.at[kind, c], recv_sem=far_recv.at[kind, c],
             device_id=(group, onward[kind]), device_id_type=pl.DeviceIdType.MESH,
         )
 
     def pass_copy(kind, c, k):
-        block = far.at[kind, group, pl.ds(c * piece, piece)]
         return pltpu.make_async_remote_copy(
-            src_ref=block, dst_ref=block,
+            src_ref=own_piece(kind, c), dst_ref=own_piece(kind, c),
             send_sem=pass_send.at[kind, c, k], recv_sem=pass_recv.at[kind, c, k],
             device_id=(peer(k), place), device_id_type=pl.DeviceIdType.MESH,
         )
-
-    def sender(k):
-        return lax.rem(group + group_width - k, group_width)
 
     for kind in (TEXT, IMAGE):
         loads(kind).start()
@@ -87,20 +88,19 @@
     factor, offset = scale[0], shift[0]
     outputs = (grad_images, grad_texts)
 
-    def meet(kind, block, diagonal=False, first=False):
-        own = near[1 - kind, group]
+    def meet(kind, block, first=False):
         z = lax.dot_general(
-            block, own, (((1,), (1,)), ((), ())), preferred_element_type=jnp.float32
+            block, own(1 - kind)[...], (((1,), (1,)), ((), ())), preferred_element_type=jnp.float32
         )
         z = factor * z + offset
-        if diagonal:
-            same = lax.broadcasted_iota(jnp.int32, z.shape, 0) == lax.broadcasted_iota(
-                jnp.int32, z.shape, 1
+        if first:
+            same = lax.broadcasted_iota(jnp.int32, z.shape, 0) == (
+                lax.broadcasted_iota(jnp.int32, z.shape, 1) + group * rows
             )
             z = jnp.where(same, -z, z)
         small = jnp.exp(-jnp.abs(z))
         slopes = factor * (jnp.where(z >= 0, 1.0, small) / (1.0 + small))
-        if diagonal:
+        if first:
             slopes = jnp.where(same, -slopes, slopes)
         if kind == TEXT:
             loss = jnp.sum(jnp.maximum(z, 0.0) + jnp.log1p(small), axis=0, keepdims=True)
@@ -114,33 +114,23 @@
 
     for kind in (TEXT, IMAGE):
         loads(kind).wait()
-    for kind in (TEXT, IMAGE):
-        meet(kind, near[kind, group], diagonal=True, first=True)
-
-    def meet_near(k):
-        for kind in (TEXT, IMAGE):
-            near_copy(kind, k).wait_recv()
-            meet(kind, near[kind, sender(k)])
-
-    over_peers(meet_near)
-
-    def meet_passed(c):
-        def one(k):
-            for kind in (TEXT, IMAGE):
-                pass_copy(kind, c, k).wait_recv()
-                meet(kind, far[kind, sender(k), pl.ds(c * piece, piece)])
-
-        over_peers(one)
+        over_peers(lambda k: near_copy(kind, k).wait_recv())
+    for kind in (TEXT, IMAGE):
+        meet(kind, near[kind], first=True)
+
+    def meet_far(c):
+        for kind in (TEXT, IMAGE):
+            over_peers(lambda k: pass_copy(kind, c, k).wait_recv())
+        for kind in (TEXT, IMAGE):
+            meet(kind, far[kind, c])
 
     for c in range(PIECES):
         for kind in (TEXT, IMAGE):
             far_copy(kind, c).wait_recv()
             over_peers(lambda k: pass_copy(kind, c, k).start())
         if c > 0:
-            meet_passed(c - 1)
-        for kind in (TEXT, IMAGE):
-            meet(kind, far[kind, group, pl.ds(c * piece, piece)])
-    meet_passed(PIECES - 1)
+            meet_far(c - 1)
+    meet_far(PIECES - 1)
     row_loss[...] = row_loss[...] / (SPAN * group_width * rows)
 
     for kind in (TEXT, IMAGE):
@@ -181,8 +171,8 @@
         + [pl.BlockSpec(memory_space=pltpu.SMEM)] * 2,
         out_specs=[pl.BlockSpec(memory_space=pltpu.VMEM)] * 3,
         scratch_shapes=[
-            pltpu.VMEM((2, group_width, rows, width), images.dtype),
-            pltpu.VMEM((2, group_width, rows, width), images.dtype),
+            pltpu.VMEM((2, group_width * rows, width), images.dtype),
+            pltpu.VMEM((2, PIECES, group_width * rows // PIECES, width), images.dtype),
             pltpu.SemaphoreType.DMA((2,)),
             pltpu.SemaphoreType.DMA((2, group_width)),
             pltpu.SemaphoreType.DMA((2, group_width)),

time: 24.6 us -> 23.4 us (0.951)
  Pallas kernels: 22.4 us -> 21.3 us
    pallas_call x1, Pallas kernels: 21.4 us -> 20.3 us  [shards(): pl.pallas_call(functools.partial(kernel, group_width, cycle), out_shape=s...]
where the time goes in v3:
time: 23.4 us; the launch traced here: 23.3 us
  Pallas kernels  21.3 us (91%)
  between operations  1.93 us (8%)
    pallas_call x1, Pallas kernels, shards(): pl.pallas_call(functools.partial(kernel, group_width, cycle), out_shape=s...  20.3 us
    pallas_call x1, Pallas kernels, shards(): pl.pallas_call(store, out_shape=shapes, in_specs=[pl.BlockSpec(memory_spa...  1.04 us

profile of v3, /device:TPU:3, one launch (start us, length us, event | category | flops | bytes accessed | tf_op | source)
XLA Modules:
  0.0 23.3 jit_solution(12071416398989557131)
XLA Ops:
  1.9 20.3 %shard_map.67 = (f32[128,1152]{1,0:T(8,128)S(1)}, f32[128,1152]{1,0:T(8,128)S(1)}, f32[1,128]{1,0:T(1,128)S(1)}) custom-call(bf16[128,1152]{1,0:T(8,128)(2,1)} %images.1, bf16[128,1152]{1,0:T(8,128)(2,1)} %texts.1, f32[1]{0:T(128)S(6)} %copy.7.scale, f32[1]{0:T(128)S(6)} %copy.8.shift), custom_call_target="tpu_custom_call" | custom-call | flops 603979776 | bytes 2359296 | tf_op jit(solution)/shard_map/pallas_call | solution.py:167
  22.2 1.0 %shard_map.68 = (f32[128,1152]{1,0:T(8,128)}, f32[128,1152]{1,0:T(8,128)}, f32[1,128]{1,0:T(1,128)}) custom-call(f32[128,1152]{1,0:T(8,128)S(1)} %get-tuple-element.9.refs_0_, f32[128,1152]{1,0:T(8,128)S(1)} %get-tuple-element.10.refs_1_, f32[1,128]{1,0:T(1,128)S(1)} %get-tuple-element.11.refs_2_), custom_call_target="tpu_custom_call" | custom-call | bytes 2359296 | tf_op jit(solution)/shard_map/pallas_call | solution.py:196

commit v4 on v3

--- a/solution.py
+++ b/solution.py
@@ -9,6 +9,7 @@
 
 SPAN = 2
 PIECES = 4
+WINDOW = 2
 TEXT, IMAGE = 0, 1
 
 
@@ -79,7 +80,7 @@
     over_peers(greet)
     pl.semaphore_wait(barrier, group_width + 1)
 
-    for c in range(PIECES):
+    for c in range(WINDOW):
         for kind in (TEXT, IMAGE):
             far_copy(kind, c).start()
     for kind in (TEXT, IMAGE):
@@ -128,13 +129,17 @@
         for kind in (TEXT, IMAGE):
             far_copy(kind, c).wait_recv()
             over_peers(lambda k: pass_copy(kind, c, k).start())
+        if c + WINDOW < PIECES:
+            for kind in (TEXT, IMAGE):
+                far_copy(kind, c).wait_send()
+                far_copy(kind, c + WINDOW).start()
         if c > 0:
             meet_far(c - 1)
     meet_far(PIECES - 1)
     row_loss[...] = row_loss[...] / (SPAN * group_width * rows)
 
     for kind in (TEXT, IMAGE):
-        for c in range(PIECES):
+        for c in range(PIECES - WINDOW, PIECES):
             far_copy(kind, c).wait_send()
 
     def sent(k):

time: 23.4 us -> 26 us (1.11)
  the two profiles are of different devices: /device:TPU:3 before, /device:TPU:0 now
where the time goes in v4:
time: 26 us; the launch traced here: 25.9 us
  Pallas kernels  23.9 us (92%)
  between operations  1.93 us (7%)
    pallas_call x1, Pallas kernels, shards(): pl.pallas_call(functools.partial(kernel, group_width, cycle), out_shape=s...  22.9 us
    pallas_call x1, Pallas kernels, shards(): pl.pallas_call(store, out_shape=shapes, in_specs=[pl.BlockSpec(memory_spa...  1.04 us

profile of v4, /device:TPU:0, one launch (start us, length us, event | category | flops | bytes accessed | tf_op | source)
XLA Modules:
  0.0 25.9 jit_solution(16809380327949860077)
XLA Ops:
  1.9 22.9 %shard_map.67 = (f32[128,1152]{1,0:T(8,128)S(1)}, f32[128,1152]{1,0:T(8,128)S(1)}, f32[1,128]{1,0:T(1,128)S(1)}) custom-call(bf16[128,1152]{1,0:T(8,128)(2,1)} %images.1, bf16[128,1152]{1,0:T(8,128)(2,1)} %texts.1, f32[1]{0:T(128)S(6)} %copy.7.scale, f32[1]{0:T(128)S(6)} %copy.8.shift), custom_call_target="tpu_custom_call" | custom-call | flops 603979776 | bytes 2359296 | tf_op jit(solution)/shard_map/pallas_call | solution.py:172
  24.8 1.0 %shard_map.68 = (f32[128,1152]{1,0:T(8,128)}, f32[128,1152]{1,0:T(8,128)}, f32[1,128]{1,0:T(1,128)}) custom-call(f32[128,1152]{1,0:T(8,128)S(1)} %get-tuple-element.9.refs_0_, f32[128,1152]{1,0:T(8,128)S(1)} %get-tuple-element.10.refs_1_, f32[1,128]{1,0:T(1,128)S(1)} %get-tuple-element.11.refs_2_), custom_call_target="tpu_custom_call" | custom-call | bytes 2359296 | tf_op jit(solution)/shard_map/pallas_call | solution.py:201

commit v5 on v3

--- a/solution.py
+++ b/solution.py
@@ -8,8 +8,8 @@
 from jax.sharding import PartitionSpec as P
 
 SPAN = 2
-PIECES = 4
 TEXT, IMAGE = 0, 1
+EIGHTHS = ((4, 4), (2, 2, 2, 1, 1))
 
 
 def kernel(
@@ -19,7 +19,12 @@
     group, place = lax.axis_index("group"), lax.axis_index("blk")
     after, before = lax.rem(place + 1, cycle), lax.rem(place + cycle - 1, cycle)
     rows = images.shape[0]
-    piece = rows // PIECES
+    travel = []
+    for kind in (TEXT, IMAGE):
+        start = 0
+        for number, eighths in enumerate(EIGHTHS[kind]):
+            travel.append((kind, number, start, eighths * rows // 8))
+            start += eighths * rows // 8
     sources = (texts, images)
     onward = (after, before)
 
@@ -36,8 +41,14 @@
     def own(kind):
         return near.at[kind, pl.ds(pl.multiple_of(group * rows, rows), rows)]
 
-    def own_piece(kind, c):
-        return far.at[kind, c, pl.ds(pl.multiple_of(group * piece, piece), piece)]
+    def whole_piece(part):
+        kind, _, start, size = part
+        return far.at[kind, pl.ds(group_width * start, group_width * size)]
+
+    def own_piece(part):
+        kind, _, start, size = part
+        offset = pl.multiple_of(group_width * start + group * size, size)
+        return far.at[kind, pl.ds(offset, size)]
 
     def loads(kind):
         return pltpu.make_async_copy(sources[kind], own(kind), load_sem.at[kind])
@@ -49,16 +60,18 @@
             device_id=(peer(k), place), device_id_type=pl.DeviceIdType.MESH,
         )
 
-    def far_copy(kind, c):
+    def far_copy(part):
+        kind, c, start, size = part
         return pltpu.make_async_remote_copy(
-            src_ref=sources[kind].at[pl.ds(c * piece, piece)], dst_ref=own_piece(kind, c),
+            src_ref=sources[kind].at[pl.ds(start, size)], dst_ref=own_piece(part),
             send_sem=far_send.at[kind, c], recv_sem=far_recv.at[kind, c],
             device_id=(group, onward[kind]), device_id_type=pl.DeviceIdType.MESH,
         )
 
-    def pass_copy(kind, c, k):
+    def pass_copy(part, k):
+        kind, c, _, _ = part
         return pltpu.make_async_remote_copy(
-            src_ref=own_piece(kind, c), dst_ref=own_piece(kind, c),
+            src_ref=own_piece(part), dst_ref=own_piece(part),
             send_sem=pass_send.at[kind, c, k], recv_sem=pass_recv.at[kind, c, k],
             device_id=(peer(k), place), device_id_type=pl.DeviceIdType.MESH,
         )
@@ -79,11 +92,11 @@
     over_peers(greet)
     pl.semaphore_wait(barrier, group_width + 1)
 
-    for c in range(PIECES):
-        for kind in (TEXT, IMAGE):
-            far_copy(kind, c).start()
+    far_copy(travel[0]).start()
     for kind in (TEXT, IMAGE):
         over_peers(lambda k: near_copy(kind, k).start())
+    for part in travel[1:]:
+        far_copy(part).start()
 
     factor, offset = scale[0], shift[0]
     outputs = (grad_images, grad_texts)
@@ -118,30 +131,28 @@
     for kind in (TEXT, IMAGE):
         meet(kind, near[kind], first=True)
 
-    def meet_far(c):
-        for kind in (TEXT, IMAGE):
-            over_peers(lambda k: pass_copy(kind, c, k).wait_recv())
-        for kind in (TEXT, IMAGE):
-            meet(kind, far[kind, c])
-
-    for c in range(PIECES):
-        for kind in (TEXT, IMAGE):
-            far_copy(kind, c).wait_recv()
-            over_peers(lambda k: pass_copy(kind, c, k).start())
-        if c > 0:
-            meet_far(c - 1)
-    meet_far(PIECES - 1)
+    def meet_far(part):
+        over_peers(lambda k: pass_copy(part, k).wait_recv())
+        meet(part[0], whole_piece(part)[...])
+
+    earlier = None
+    for part in travel:
+        far_copy(part).wait_recv()
+        over_peers(lambda k: pass_copy(part, k).start())
+        if earlier is not None:
+            meet_far(earlier)
+        earlier = part
+    meet_far(earlier)
     row_loss[...] = row_loss[...] / (SPAN * group_width * rows)
 
-    for kind in (TEXT, IMAGE):
-        for c in range(PIECES):
-            far_copy(kind, c).wait_send()
+    for part in travel:
+        far_copy(part).wait_send()
 
     def sent(k):
         for kind in (TEXT, IMAGE):
             near_copy(kind, k).wait_send()
-            for c in range(PIECES):
-                pass_copy(kind, c, k).wait_send()
+        for part in travel:
+            pass_copy(part, k).wait_send()
 
     over_peers(sent)
 
@@ -159,6 +170,7 @@
 def shards(group_width, cycle, images, texts, scale, shift):
     rows, width = images.shape
     flops = 4 * 2 * rows * SPAN * group_width * rows * width
+    most = max(len(pieces) for pieces in EIGHTHS)
     shapes = (
         jax.ShapeDtypeStruct((rows, width), jnp.float32),
         jax.ShapeDtypeStruct((rows, width), jnp.float32),
@@ -172,14 +184,14 @@
         out_specs=[pl.BlockSpec(memory_space=pltpu.VMEM)] * 3,
         scratch_shapes=[
             pltpu.VMEM((2, group_width * rows, width), images.dtype),
-            pltpu.VMEM((2, PIECES, group_width * rows // PIECES, width), images.dtype),
+            pltpu.VMEM((2, group_width * rows, width), images.dtype),
             pltpu.SemaphoreType.DMA((2,)),
             pltpu.SemaphoreType.DMA((2, group_width)),
             pltpu.SemaphoreType.DMA((2, group_width)),
-            pltpu.SemaphoreType.DMA((2, PIECES)),
-            pltpu.SemaphoreType.DMA((2, PIECES)),
-            pltpu.SemaphoreType.DMA((2, PIECES, group_width)),
-            pltpu.SemaphoreType.DMA((2, PIECES, group_width)),
+            pltpu.SemaphoreType.DMA((2, most)),
+            pltpu.SemaphoreType.DMA((2, most)),
+            pltpu.SemaphoreType.DMA((2, most, group_width)),
+            pltpu.SemaphoreType.DMA((2, most, group_width)),
         ],
         compiler_params=pltpu.CompilerParams(
             collective_id=0, has_side_effects=True, vmem_limit_bytes=32 << 20

time: 23.4 us -> 26.6 us (1.14)
  Pallas kernels: 21.3 us -> 24.5 us
    pallas_call x1, Pallas kernels: 20.3 us -> 23.5 us  [shards(): pl.pallas_call(functools.partial(kernel, group_width, cycle), out_shape=s...]
where the time goes in v5:
time: 26.6 us; the launch traced here: 26.5 us
  Pallas kernels  24.5 us (92%)
  between operations  1.93 us (7%)
    pallas_call x1, Pallas kernels, shards(): pl.pallas_call(functools.partial(kernel, group_width, cycle), out_shape=s...  23.5 us
    pallas_call x1, Pallas kernels, shards(): pl.pallas_call(store, out_shape=shapes, in_specs=[pl.BlockSpec(memory_spa...  1.04 us

profile of v5, /device:TPU:3, one launch (start us, length us, event | category | flops | bytes accessed | tf_op | source)
XLA Modules:
  0.0 26.5 jit_solution(3253494428067720003)
XLA Ops:
  1.9 23.5 %shard_map.67 = (f32[128,1152]{1,0:T(8,128)S(1)}, f32[128,1152]{1,0:T(8,128)S(1)}, f32[1,128]{1,0:T(1,128)S(1)}) custom-call(bf16[128,1152]{1,0:T(8,128)(2,1)} %images.1, bf16[128,1152]{1,0:T(8,128)(2,1)} %texts.1, f32[1]{0:T(128)S(6)} %copy.7.scale, f32[1]{0:T(128)S(6)} %copy.8.shift), custom_call_target="tpu_custom_call" | custom-call | flops 603979776 | bytes 2359296 | tf_op jit(solution)/shard_map/pallas_call | solution.py:179
  25.4 1.0 %shard_map.68 = (f32[128,1152]{1,0:T(8,128)}, f32[128,1152]{1,0:T(8,128)}, f32[1,128]{1,0:T(1,128)}) custom-call(f32[128,1152]{1,0:T(8,128)S(1)} %get-tuple-element.9.refs_0_, f32[128,1152]{1,0:T(8,128)S(1)} %get-tuple-element.10.refs_1_, f32[1,128]{1,0:T(1,128)S(1)} %get-tuple-element.11.refs_2_), custom_call_target="tpu_custom_call" | custom-call | bytes 2359296 | tf_op jit(solution)/shard_map/pallas_call | solution.py:208

commit v6 on v3

v6 whole, which is shorter than its diff:
```python
import functools

import jax
import jax.numpy as jnp
from jax import lax
from jax.experimental import pallas as pl
from jax.experimental.pallas import tpu as pltpu
from jax.sharding import PartitionSpec as P

SPAN = 2
TEXT, IMAGE = 0, 1
VIA, DIRECT = (2, 2, 2, 2), (2, 2, 2, 1, 1)
TURNS = "r0 T0 r1 I0 r2 v0 r3 v1 V0 v2 V1 d0 v3 V2 D0 d1 V3 d2 D1 d3 D2 d4 D3 D4"


def pieces(eighths, rows):
    parts, start = [], 0
    for share in eighths:
        parts.append((start, share * rows // 8))
        start += share * rows // 8
    return parts


def kernel(
    group_width, cycle, images, texts, scale, shift, grads, row_loss,
    near, relay, via, direct, losses, load_sem, near_send, near_recv, out_send, out_recv,
    on_send, on_recv, via_send, via_recv, pass_send, pass_recv,
):
    group, place = lax.axis_index("group"), lax.axis_index("blk")
    odd = lax.rem(place, 2)
    partner = place + 1 - 2 * odd
    onward = lax.rem(place + cycle + 2 - 4 * odd, cycle)
    behind = lax.rem(place + cycle - 2 + 4 * odd, cycle)
    via_kind, direct_kind = odd, 1 - odd
    rows = images.shape[0]
    via_parts, direct_parts = pieces(VIA, rows), pieces(DIRECT, rows)

    def peer(k):
        return lax.rem(group + k, group_width)

    def over_peers(body):
        if group_width <= 2:
            for k in range(1, group_width):
                body(k)
        else:
            pl.loop(1, group_width)(body)

    def remote(src, dst, send, recv, device):
        return pltpu.make_async_remote_copy(
            src_ref=src, dst_ref=dst, send_sem=send, recv_sem=recv,
            device_id=device, device_id_type=pl.DeviceIdType.MESH,
        )

    def own(kind, start=0, size=rows):
        return near.at[kind, pl.ds(pl.multiple_of(group * rows + start, size), size)]

    def mine(block, part):
        start, size = part
        return block.at[pl.ds(pl.multiple_of(group_width * start + group * size, size), size)]

    def load(kind):
        return pltpu.make_async_copy((texts, images)[kind], own(kind), load_sem.at[kind])

    def near_copy(kind, k):
        return remote(
            own(kind), own(kind), near_send.at[kind, k], near_recv.at[kind, k], (peer(k), place)
        )

    def first_copy(c):
        start, size = via_parts[c]
        return remote(
            own(1 - odd, start, size), relay.at[pl.ds(start, size)],
            out_send.at[c], out_recv.at[c], (group, partner),
        )

    def onward_copy(c):
        start, size = via_parts[c]
        return remote(
            relay.at[pl.ds(start, size)], mine(via, via_parts[c]),
            on_send.at[c], on_recv.at[c], (group, onward),
        )

    def direct_copy(c):
        start, size = direct_parts[c]
        return remote(
            own(odd, start, size), mine(direct, direct_parts[c]),
            via_send.at[c], via_recv.at[c], (group, partner),
        )

    def pass_copy(which, c, k):
        block = mine(direct, direct_parts[c]) if which else mine(via, via_parts[c])
        return remote(
            block, block, pass_send.at[which, c, k], pass_recv.at[which, c, k], (peer(k), place)
        )

    for kind in (TEXT, IMAGE):
        load(kind).start()
    barrier = pltpu.get_barrier_semaphore()

    def greet(device):
        pl.semaphore_signal(
            barrier, inc=1, device_id=device, device_id_type=pl.DeviceIdType.MESH
        )

    greet((group, behind))
    greet((group, partner))
    over_peers(lambda k: greet((peer(k), place)))
    for kind in (TEXT, IMAGE):
        load(kind).wait()
    pl.semaphore_wait(barrier, group_width + 1)

    for c in range(len(VIA)):
        first_copy(c).start()
    for kind in (TEXT, IMAGE):
        over_peers(lambda k: near_copy(kind, k).start())
    for c in range(len(DIRECT)):
        direct_copy(c).start()

    factor, offset = scale[0], shift[0]

    def meet(kind, block, first=False):
        z = lax.dot_general(
            block, own(1 - kind)[...], (((1,), (1,)), ((), ())),
            preferred_element_type=jnp.float32,
        )
        z = factor * z + offset
        if first:
            same = lax.broadcasted_iota(jnp.int32, z.shape, 0) == (
                lax.broadcasted_iota(jnp.int32, z.shape, 1) + group * rows
            )
            z = jnp.where(same, -z, z)
        small = jnp.exp(-jnp.abs(z))
        slopes = factor * (jnp.where(z >= 0, 1.0, small) / (1.0 + small))
        if first:
            slopes = jnp.where(same, -slopes, slopes)
        loss = jnp.sum(jnp.maximum(z, 0.0) + jnp.log1p(small), axis=0, keepdims=True)
        grad = lax.dot_general(
            slopes.astype(jnp.bfloat16), block, (((0,), (0,)), ((), ())),
            preferred_element_type=jnp.float32,
        )
        losses[kind] = loss if first else losses[kind] + loss
        grads[kind] = grad if first else grads[kind] + grad

    for turn in TURNS.split():
        what, c = turn[0], int(turn[1:])
        if what == "r":
            first_copy(c).wait_recv()
            onward_copy(c).start()
        elif what in "vd":
            (direct_copy if what == "d" else onward_copy)(c).wait_recv()
            over_peers(lambda k: pass_copy(int(what == "d"), c, k).start())
        elif what in "VD":
            over_peers(lambda k: pass_copy(int(what == "D"), c, k).wait_recv())
            block, kind = (direct, direct_kind) if what == "D" else (via, via_kind)
            start, size = (direct_parts if what == "D" else via_parts)[c]
            meet(kind, block[pl.ds(group_width * start, group_width * size)])
        else:
            kind = TEXT if what == "T" else IMAGE
            if kind == TEXT:
                for each in (TEXT, IMAGE):
                    over_peers(lambda k: near_copy(each, k).wait_recv())
            meet(kind, near[kind], first=True)
    row_loss[...] = losses[TEXT] / (SPAN * group_width * rows)

    for c in range(len(VIA)):
        first_copy(c).wait_send()
        onward_copy(c).wait_send()
    for c in range(len(DIRECT)):
        direct_copy(c).wait_send()

    def sent(k):
        for kind in (TEXT, IMAGE):
            near_copy(kind, k).wait_send()
        for which, count in ((0, len(VIA)), (1, len(DIRECT))):
            for c in range(count):
                pass_copy(which, c, k).wait_send()

    over_peers(sent)


def store(grads, held_loss, grad_images, grad_texts, row_loss, sem):
    moves = ((grads.at[0], grad_images), (grads.at[1], grad_texts), (held_loss, row_loss))
    copies = [pltpu.make_async_copy(a, b, sem.at[i]) for i, (a, b) in enumerate(moves)]
    for copy in copies:
        copy.start()
    for copy in copies:
        copy.wait()


def shards(group_width, cycle, images, texts, scale, shift):
    rows, width = images.shape
    flops = 4 * 2 * rows * SPAN * group_width * rows * width
    most = max(len(VIA), len(DIRECT))
    results = pl.pallas_call(
        functools.partial(kernel, group_width, cycle),
        out_shape=(
            jax.ShapeDtypeStruct((2, rows, width), jnp.float32),
            jax.ShapeDtypeStruct((1, rows), jnp.float32),
        ),
        in_specs=[pl.BlockSpec(memory_space=pltpu.HBM)] * 2
        + [pl.BlockSpec(memory_space=pltpu.SMEM)] * 2,
        out_specs=[pl.BlockSpec(memory_space=pltpu.VMEM)] * 2,
        scratch_shapes=[
            pltpu.VMEM((2, group_width * rows, width), images.dtype),
            pltpu.VMEM((rows, width), images.dtype),
            pltpu.VMEM((group_width * rows, width), images.dtype),
            pltpu.VMEM((group_width * rows, width), images.dtype),
            pltpu.VMEM((2, 1, rows), jnp.float32),
            pltpu.SemaphoreType.DMA((2,)),
            pltpu.SemaphoreType.DMA((2, group_width)),
            pltpu.SemaphoreType.DMA((2, group_width)),
        ]
        + [pltpu.SemaphoreType.DMA((most,))] * 6
        + [pltpu.SemaphoreType.DMA((2, most, group_width))] * 2,
        compiler_params=pltpu.CompilerParams(
            collective_id=0, has_side_effects=True, vmem_limit_bytes=32 << 20
        ),
        cost_estimate=pl.CostEstimate(
            flops=flops, bytes_accessed=16 * rows * width, transcendentals=0
        ),
    )(
        pltpu.with_memory_space_constraint(images, pltpu.HBM),
        pltpu.with_memory_space_constraint(texts, pltpu.HBM),
        scale,
        shift,
    )
    grad_images, grad_texts, row_loss = pl.pallas_call(
        store,
        out_shape=(
            jax.ShapeDtypeStruct((rows, width), jnp.float32),
            jax.ShapeDtypeStruct((rows, width), jnp.float32),
            jax.ShapeDtypeStruct((1, rows), jnp.float32),
        ),
        in_specs=[pl.BlockSpec(memory_space=pltpu.VMEM)] * 2,
        out_specs=[pl.BlockSpec(memory_space=pltpu.HBM)] * 3,
        scratch_shapes=[pltpu.SemaphoreType.DMA((3,))],
        compiler_params=pltpu.CompilerParams(vmem_limit_bytes=8 << 20),
        cost_estimate=pl.CostEstimate(
            flops=0, bytes_accessed=16 * rows * width, transcendentals=0
        ),
    )(*results)
    return grad_images, grad_texts, row_loss.reshape(rows)


def solution(mesh):
    placed = (P(("group", "blk"), None), P(("group", "blk"), None), P(), P())
    return jax.shard_map(
        functools.partial(shards, mesh.shape["group"], mesh.shape["blk"]),
        mesh=mesh,
        in_specs=placed,
        out_specs=(P(("group", "blk"), None), P(("group", "blk"), None), P(("group", "blk"))),
        check_vma=False,
    )
```

time: 23.4 us -> 27.4 us (1.17)
  the two profiles are of different devices: /device:TPU:3 before, /device:TPU:0 now
where the time goes in v6:
time: 27.4 us; the launch traced here: 27.3 us
  Pallas kernels  25.3 us (92%)
  between operations  1.93 us (7%)
    pallas_call x1, Pallas kernels, shards(): pl.pallas_call(functools.partial(kernel, group_width, cycle), out_shape=(...  24.3 us
    pallas_call x1, Pallas kernels, shards(): pl.pallas_call(store, out_shape=(jax.ShapeDtypeStruct((rows, width), jnp....  1.04 us

profile of v6, /device:TPU:0, one launch (start us, length us, event | category | flops | bytes accessed | tf_op | source)
XLA Modules:
  0.0 27.3 jit_solution(15721753398998753068)
XLA Ops:
  1.9 24.3 %shard_map.67 = (f32[2,128,1152]{2,1,0:T(8,128)S(1)}, f32[1,128]{1,0:T(1,128)S(1)}) custom-call(bf16[128,1152]{1,0:T(8,128)(2,1)} %images.1, bf16[128,1152]{1,0:T(8,128)(2,1)} %texts.1, f32[1]{0:T(128)S(6)} %copy.7.scale, f32[1]{0:T(128)S(6)} %copy.8.shift), custom_call_target="tpu_custom_call" | custom-call | flops 603979776 | bytes 2359296 | tf_op jit(solution)/shard_map/pallas_call | solution.py:194
  26.2 1.0 %shard_map.68 = (f32[128,1152]{1,0:T(8,128)}, f32[128,1152]{1,0:T(8,128)}, f32[1,128]{1,0:T(1,128)}) custom-call(f32[2,128,1152]{2,1,0:T(8,128)S(1)} %get-tuple-element.8.grads, f32[1,128]{1,0:T(1,128)S(1)} %get-tuple-element.9.held_loss), custom_call_target="tpu_custom_call" | custom-call | bytes 2359296 | tf_op jit(solution)/shard_map/pallas_call | solution.py:227

commit v7 on v5

--- a/solution.py
+++ b/solution.py
@@ -9,7 +9,7 @@
 
 SPAN = 2
 TEXT, IMAGE = 0, 1
-EIGHTHS = ((4, 4), (2, 2, 2, 1, 1))
+EIGHTHS = (2, 2, 2, 1, 1)
 
 
 def kernel(
@@ -20,11 +20,11 @@
     after, before = lax.rem(place + 1, cycle), lax.rem(place + cycle - 1, cycle)
     rows = images.shape[0]
     travel = []
-    for kind in (TEXT, IMAGE):
-        start = 0
-        for number, eighths in enumerate(EIGHTHS[kind]):
-            travel.append((kind, number, start, eighths * rows // 8))
-            start += eighths * rows // 8
+    start = 0
+    for number, eighths in enumerate(EIGHTHS):
+        size = eighths * rows // 8
+        travel += [(kind, number, start, size) for kind in (TEXT, IMAGE)]
+        start += size
     sources = (texts, images)
     onward = (after, before)
 
@@ -92,10 +92,9 @@
     over_peers(greet)
     pl.semaphore_wait(barrier, group_width + 1)
 
-    far_copy(travel[0]).start()
     for kind in (TEXT, IMAGE):
         over_peers(lambda k: near_copy(kind, k).start())
-    for part in travel[1:]:
+    for part in travel:
         far_copy(part).start()
 
     factor, offset = scale[0], shift[0]
@@ -131,18 +130,22 @@
     for kind in (TEXT, IMAGE):
         meet(kind, near[kind], first=True)
 
-    def meet_far(part):
-        over_peers(lambda k: pass_copy(part, k).wait_recv())
-        meet(part[0], whole_piece(part)[...])
-
-    earlier = None
-    for part in travel:
+    def meet_far(*parts):
+        for part in parts:
+            over_peers(lambda k: pass_copy(part, k).wait_recv())
+        for part in parts:
+            meet(part[0], whole_piece(part)[...])
+
+    def pass_on(part):
         far_copy(part).wait_recv()
         over_peers(lambda k: pass_copy(part, k).start())
-        if earlier is not None:
-            meet_far(earlier)
-        earlier = part
-    meet_far(earlier)
+
+    for i in range(0, len(travel), 2):
+        pass_on(travel[i])
+        pass_on(travel[i + 1])
+        if i > 0:
+            meet_far(travel[i - 2], travel[i - 1])
+    meet_far(travel[-2], travel[-1])
     row_loss[...] = row_loss[...] / (SPAN * group_width * rows)
 
     for part in travel:
@@ -170,7 +173,6 @@
 def shards(group_width, cycle, images, texts, scale, shift):
     rows, width = images.shape
     flops = 4 * 2 * rows * SPAN * group_width * rows * width
-    most = max(len(pieces) for pieces in EIGHTHS)
     shapes = (
         jax.ShapeDtypeStruct((rows, width), jnp.float32),
         jax.ShapeDtypeStruct((rows, width), jnp.float32),
@@ -188,10 +190,10 @@
             pltpu.SemaphoreType.DMA((2,)),
             pltpu.SemaphoreType.DMA((2, group_width)),
             pltpu.SemaphoreType.DMA((2, group_width)),
-            pltpu.SemaphoreType.DMA((2, most)),
-            pltpu.SemaphoreType.DMA((2, most)),
-            pltpu.SemaphoreType.DMA((2, most, group_width)),
-            pltpu.SemaphoreType.DMA((2, most, group_width)),
+            pltpu.SemaphoreType.DMA((2, len(EIGHTHS))),
+            pltpu.SemaphoreType.DMA((2, len(EIGHTHS))),
+            pltpu.SemaphoreType.DMA((2, len(EIGHTHS), group_width)),
+            pltpu.SemaphoreType.DMA((2, len(EIGHTHS), group_width)),
         ],
         compiler_params=pltpu.CompilerParams(
             collective_id=0, has_side_effects=True, vmem_limit_bytes=32 << 20

time: 26.6 us -> 23.9 us (0.90)
  Pallas kernels: 24.5 us -> 21.8 us
    pallas_call x1, Pallas kernels: 23.5 us -> 20.8 us  [shards(): pl.pallas_call(functools.partial(kernel, group_width, cycle), out_shape=s...]
where the time goes in v7:
time: 23.9 us; the launch traced here: 23.7 us
  Pallas kernels  21.8 us (91%)
  between operations  1.93 us (8%)
    pallas_call x1, Pallas kernels, shards(): pl.pallas_call(functools.partial(kernel, group_width, cycle), out_shape=s...  20.8 us
    pallas_call x1, Pallas kernels, shards(): pl.pallas_call(store, out_shape=shapes, in_specs=[pl.BlockSpec(memory_spa...  1.04 us

profile of v7, /device:TPU:3, one launch (start us, length us, event | category | flops | bytes accessed | tf_op | source)
XLA Modules:
  0.0 23.7 jit_solution(6796055611849685687)
XLA Ops:
  1.9 20.8 %shard_map.67 = (f32[128,1152]{1,0:T(8,128)S(1)}, f32[128,1152]{1,0:T(8,128)S(1)}, f32[1,128]{1,0:T(1,128)S(1)}) custom-call(bf16[128,1152]{1,0:T(8,128)(2,1)} %images.1, bf16[128,1152]{1,0:T(8,128)(2,1)} %texts.1, f32[1]{0:T(128)S(6)} %copy.7.scale, f32[1]{0:T(128)S(6)} %copy.8.shift), custom_call_target="tpu_custom_call" | custom-call | flops 603979776 | bytes 2359296 | tf_op jit(solution)/shard_map/pallas_call | solution.py:181
  22.7 1.0 %shard_map.68 = (f32[128,1152]{1,0:T(8,128)}, f32[128,1152]{1,0:T(8,128)}, f32[1,128]{1,0:T(1,128)}) custom-call(f32[128,1152]{1,0:T(8,128)S(1)} %get-tuple-element.9.refs_0_, f32[128,1152]{1,0:T(8,128)S(1)} %get-tuple-element.10.refs_1_, f32[1,128]{1,0:T(1,128)S(1)} %get-tuple-element.11.refs_2_), custom_call_target="tpu_custom_call" | custom-call | bytes 2359296 | tf_op jit(solution)/shard_map/pallas_call | solution.py:210

commit v8 on v7

--- a/solution.py
+++ b/solution.py
@@ -9,12 +9,13 @@
 
 SPAN = 2
 TEXT, IMAGE = 0, 1
-EIGHTHS = (2, 2, 2, 1, 1)
+EIGHTHS = (4, 2, 1, 1)
 
 
 def kernel(
     group_width, cycle, images, texts, scale, shift, grad_images, grad_texts, row_loss,
-    near, far, load_sem, near_send, near_recv, far_send, far_recv, pass_send, pass_recv,
+    near, far, sums, going, coming, losses, losses_in, load_sem, near_send, near_recv,
+    far_send, far_recv, sum_send, sum_recv, loss_send, loss_recv,
 ):
     group, place = lax.axis_index("group"), lax.axis_index("blk")
     after, before = lax.rem(place + 1, cycle), lax.rem(place + cycle - 1, cycle)
@@ -41,15 +42,6 @@
     def own(kind):
         return near.at[kind, pl.ds(pl.multiple_of(group * rows, rows), rows)]
 
-    def whole_piece(part):
-        kind, _, start, size = part
-        return far.at[kind, pl.ds(group_width * start, group_width * size)]
-
-    def own_piece(part):
-        kind, _, start, size = part
-        offset = pl.multiple_of(group_width * start + group * size, size)
-        return far.at[kind, pl.ds(offset, size)]
-
     def loads(kind):
         return pltpu.make_async_copy(sources[kind], own(kind), load_sem.at[kind])
 
@@ -62,17 +54,24 @@
 
     def far_copy(part):
         kind, c, start, size = part
-        return pltpu.make_async_remote_copy(
-            src_ref=sources[kind].at[pl.ds(start, size)], dst_ref=own_piece(part),
+        piece = pl.ds(start, size)
+        return pltpu.make_async_remote_copy(
+            src_ref=sources[kind].at[piece], dst_ref=far.at[kind, piece],
             send_sem=far_send.at[kind, c], recv_sem=far_recv.at[kind, c],
             device_id=(group, onward[kind]), device_id_type=pl.DeviceIdType.MESH,
         )
 
-    def pass_copy(part, k):
-        kind, c, _, _ = part
-        return pltpu.make_async_remote_copy(
-            src_ref=own_piece(part), dst_ref=own_piece(part),
-            send_sem=pass_send.at[kind, c, k], recv_sem=pass_recv.at[kind, c, k],
+    def sum_copy(kind, k):
+        return pltpu.make_async_remote_copy(
+            src_ref=going.at[kind, k], dst_ref=coming.at[kind, k],
+            send_sem=sum_send.at[kind, k], recv_sem=sum_recv.at[kind, k],
+            device_id=(peer(k), place), device_id_type=pl.DeviceIdType.MESH,
+        )
+
+    def loss_copy(k):
+        return pltpu.make_async_remote_copy(
+            src_ref=losses.at[peer(k)], dst_ref=losses_in.at[k],
+            send_sem=loss_send.at[k], recv_sem=loss_recv.at[k],
             device_id=(peer(k), place), device_id_type=pl.DeviceIdType.MESH,
         )
 
@@ -100,52 +99,79 @@
     factor, offset = scale[0], shift[0]
     outputs = (grad_images, grad_texts)
 
-    def meet(kind, block, first=False):
+    def products(block, others, diagonal=False):
         z = lax.dot_general(
-            block, own(1 - kind)[...], (((1,), (1,)), ((), ())), preferred_element_type=jnp.float32
+            block, others, (((1,), (1,)), ((), ())), preferred_element_type=jnp.float32
         )
         z = factor * z + offset
-        if first:
+        if diagonal:
             same = lax.broadcasted_iota(jnp.int32, z.shape, 0) == (
                 lax.broadcasted_iota(jnp.int32, z.shape, 1) + group * rows
             )
             z = jnp.where(same, -z, z)
         small = jnp.exp(-jnp.abs(z))
         slopes = factor * (jnp.where(z >= 0, 1.0, small) / (1.0 + small))
-        if first:
+        if diagonal:
             slopes = jnp.where(same, -slopes, slopes)
-        if kind == TEXT:
-            loss = jnp.sum(jnp.maximum(z, 0.0) + jnp.log1p(small), axis=0, keepdims=True)
-            row_loss[...] = loss if first else row_loss[...] + loss
+        loss = jnp.maximum(z, 0.0) + jnp.log1p(small)
         grad = lax.dot_general(
             slopes.astype(jnp.bfloat16), block, (((0,), (0,)), ((), ())),
             preferred_element_type=jnp.float32,
         )
-        out = outputs[kind]
-        out[...] = grad if first else out[...] + grad
+        return jnp.sum(loss, axis=0, keepdims=True), grad
+
+    def meet_near(kind):
+        loss, outputs[kind][...] = products(near[kind], own(1 - kind)[...], diagonal=True)
+        if kind == TEXT:
+            row_loss[...] = loss
+
+    def meet_far(part):
+        kind, c, start, size = part
+        far_copy(part).wait_recv()
+        loss, grad = products(far[kind, pl.ds(start, size)], near[1 - kind])
+        sums[kind] = grad if c == 0 else sums[kind] + grad
+        if kind == TEXT:
+            for s in range(group_width):
+                one = loss[:, s * rows : (s + 1) * rows]
+                one = jnp.broadcast_to(one, losses.shape[1:])
+                losses[s] = one if c == 0 else losses[s] + one
+
+    def block_of(s):
+        return pl.ds(pl.multiple_of(s * rows, rows), rows)
+
+    def send_sums(kind):
+        def one(k):
+            going[kind, k] = sums[kind, block_of(peer(k))].astype(jnp.bfloat16)
+            sum_copy(kind, k).start()
+            if kind == TEXT:
+                loss_copy(k).start()
+
+        over_peers(one)
+        outputs[kind][...] += sums[kind, block_of(group)]
+        if kind == TEXT:
+            row_loss[...] += losses[group, pl.ds(0, 1)]
+
+    def take_sums(kind):
+        def one(k):
+            sum_copy(kind, k).wait_recv()
+            outputs[kind][...] += coming[kind, k].astype(jnp.float32)
+            if kind == TEXT:
+                loss_copy(k).wait_recv()
+                row_loss[...] += losses_in[k, pl.ds(0, 1)]
+
+        over_peers(one)
 
     for kind in (TEXT, IMAGE):
         loads(kind).wait()
         over_peers(lambda k: near_copy(kind, k).wait_recv())
     for kind in (TEXT, IMAGE):
-        meet(kind, near[kind], first=True)
-
-    def meet_far(*parts):
-        for part in parts:
-            over_peers(lambda k: pass_copy(part, k).wait_recv())
-        for part in parts:
-            meet(part[0], whole_piece(part)[...])
-
-    def pass_on(part):
-        far_copy(part).wait_recv()
-        over_peers(lambda k: pass_copy(part, k).start())
-
-    for i in range(0, len(travel), 2):
-        pass_on(travel[i])
-        pass_on(travel[i + 1])
-        if i > 0:
-            meet_far(travel[i - 2], travel[i - 1])
-    meet_far(travel[-2], travel[-1])
+        meet_near(kind)
+    for part in travel:
+        meet_far(part)
+        if part[1] == len(EIGHTHS) - 1:
+            send_sums(part[0])
+    for kind in (TEXT, IMAGE):
+        take_sums(kind)
     row_loss[...] = row_loss[...] / (SPAN * group_width * rows)
 
     for part in travel:
@@ -154,8 +180,8 @@
     def sent(k):
         for kind in (TEXT, IMAGE):
             near_copy(kind, k).wait_send()
-        for part in travel:
-            pass_copy(part, k).wait_send()
+            sum_copy(kind, k).wait_send()
+        loss_copy(k).wait_send()
 
     over_peers(sent)
 
@@ -186,14 +212,21 @@
         out_specs=[pl.BlockSpec(memory_space=pltpu.VMEM)] * 3,
         scratch_shapes=[
             pltpu.VMEM((2, group_width * rows, width), images.dtype),
-            pltpu.VMEM((2, group_width * rows, width), images.dtype),
+            pltpu.VMEM((2, rows, width), images.dtype),
+            pltpu.VMEM((2, group_width * rows, width), jnp.float32),
+            pltpu.VMEM((2, group_width, rows, width), jnp.bfloat16),
+            pltpu.VMEM((2, group_width, rows, width), jnp.bfloat16),
+            pltpu.VMEM((group_width, 8, rows), jnp.float32),
+            pltpu.VMEM((group_width, 8, rows), jnp.float32),
             pltpu.SemaphoreType.DMA((2,)),
             pltpu.SemaphoreType.DMA((2, group_width)),
             pltpu.SemaphoreType.DMA((2, group_width)),
             pltpu.SemaphoreType.DMA((2, len(EIGHTHS))),
             pltpu.SemaphoreType.DMA((2, len(EIGHTHS))),
-            pltpu.SemaphoreType.DMA((2, len(EIGHTHS), group_width)),
-            pltpu.SemaphoreType.DMA((2, len(EIGHTHS), group_width)),
+            pltpu.SemaphoreType.DMA((2, group_width)),
+            pltpu.SemaphoreType.DMA((2, group_width)),
+            pltpu.SemaphoreType.DMA((group_width,)),
+            pltpu.SemaphoreType.DMA((group_width,)),
         ],
         compiler_params=pltpu.CompilerParams(
             collective_id=0, has_side_effects=True, vmem_limit_bytes=32 << 20

time: 23.9 us -> 26.7 us (1.12)
  Pallas kernels: 21.8 us -> 24.6 us
    pallas_call x1, Pallas kernels: 20.8 us -> 23.5 us  [shards(): pl.pallas_call(functools.partial(kernel, group_width, cycle), out_shape=s...]
where the time goes in v8:
time: 26.7 us; the launch traced here: 26.5 us
  Pallas kernels  24.6 us (92%)
  between operations  1.93 us (7%)
    pallas_call x1, Pallas kernels, shards(): pl.pallas_call(functools.partial(kernel, group_width, cycle), out_shape=s...  23.5 us
    pallas_call x1, Pallas kernels, shards(): pl.pallas_call(store, out_shape=shapes, in_specs=[pl.BlockSpec(memory_spa...  1.04 us

profile of v8, /device:TPU:3, one launch (start us, length us, event | category | flops | bytes accessed | tf_op | source)
XLA Modules:
  0.0 26.5 jit_solution(14373982272285994126)
XLA Ops:
  1.9 23.5 %shard_map.67 = (f32[128,1152]{1,0:T(8,128)S(1)}, f32[128,1152]{1,0:T(8,128)S(1)}, f32[1,128]{1,0:T(1,128)S(1)}) custom-call(bf16[128,1152]{1,0:T(8,128)(2,1)} %images.1, bf16[128,1152]{1,0:T(8,128)(2,1)} %texts.1, f32[1]{0:T(128)S(6)} %copy.7.scale, f32[1]{0:T(128)S(6)} %copy.8.shift), custom_call_target="tpu_custom_call" | custom-call | flops 603979776 | bytes 2359296 | tf_op jit(solution)/shard_map/pallas_call | solution.py:207
  25.5 1.0 %shard_map.68 = (f32[128,1152]{1,0:T(8,128)}, f32[128,1152]{1,0:T(8,128)}, f32[1,128]{1,0:T(1,128)}) custom-call(f32[128,1152]{1,0:T(8,128)S(1)} %get-tuple-element.9.refs_0_, f32[128,1152]{1,0:T(8,128)S(1)} %get-tuple-element.10.refs_1_, f32[1,128]{1,0:T(1,128)S(1)} %get-tuple-element.11.refs_2_), custom_call_target="tpu_custom_call" | custom-call | bytes 2359296 | tf_op jit(solution)/shard_map/pallas_call | solution.py:243

commit v9 on v7

--- a/solution.py
+++ b/solution.py
@@ -9,7 +9,7 @@
 
 SPAN = 2
 TEXT, IMAGE = 0, 1
-EIGHTHS = (2, 2, 2, 1, 1)
+EIGHTHS = (4, 2, 1, 1)
 
 
 def kernel(
@@ -92,10 +92,10 @@
     over_peers(greet)
     pl.semaphore_wait(barrier, group_width + 1)
 
-    for kind in (TEXT, IMAGE):
-        over_peers(lambda k: near_copy(kind, k).start())
     for part in travel:
         far_copy(part).start()
+    for kind in (TEXT, IMAGE):
+        over_peers(lambda k: near_copy(kind, k).start())
 
     factor, offset = scale[0], shift[0]
     outputs = (grad_images, grad_texts)

time: 23.9 us -> 23.8 us (level)
  no operation moved by 1% of the time
where the time goes in v9:
time: 23.8 us; the launch traced here: 23.6 us
  Pallas kernels  21.7 us (91%)
  between operations  1.93 us (8%)
    pallas_call x1, Pallas kernels, shards(): pl.pallas_call(functools.partial(kernel, group_width, cycle), out_shape=s...  20.6 us
    pallas_call x1, Pallas kernels, shards(): pl.pallas_call(store, out_shape=shapes, in_specs=[pl.BlockSpec(memory_spa...  1.04 us

profile of v9, /device:TPU:3, one launch (start us, length us, event | category | flops | bytes accessed | tf_op | source)
XLA Modules:
  0.0 23.6 jit_solution(17957770684649576401)
XLA Ops:
  1.9 20.6 %shard_map.67 = (f32[128,1152]{1,0:T(8,128)S(1)}, f32[128,1152]{1,0:T(8,128)S(1)}, f32[1,128]{1,0:T(1,128)S(1)}) custom-call(bf16[128,1152]{1,0:T(8,128)(2,1)} %images.1, bf16[128,1152]{1,0:T(8,128)(2,1)} %texts.1, f32[1]{0:T(128)S(6)} %copy.7.scale, f32[1]{0:T(128)S(6)} %copy.8.shift), custom_call_target="tpu_custom_call" | custom-call | flops 603979776 | bytes 2359296 | tf_op jit(solution)/shard_map/pallas_call | solution.py:181
  22.6 1.0 %shard_map.68 = (f32[128,1152]{1,0:T(8,128)}, f32[128,1152]{1,0:T(8,128)}, f32[1,128]{1,0:T(1,128)}) custom-call(f32[128,1152]{1,0:T(8,128)S(1)} %get-tuple-element.9.refs_0_, f32[128,1152]{1,0:T(8,128)S(1)} %get-tuple-element.10.refs_1_, f32[1,128]{1,0:T(1,128)S(1)} %get-tuple-element.11.refs_2_), custom_call_target="tpu_custom_call" | custom-call | bytes 2359296 | tf_op jit(solution)/shard_map/pallas_call | solution.py:210

commit v10 on v3

--- a/solution.py
+++ b/solution.py
@@ -9,7 +9,7 @@
 
 SPAN = 2
 PIECES = 4
-TEXT, IMAGE = 0, 1
+TEXT, IMAGE, RELAY = 0, 1, 2
 
 
 def kernel(
@@ -21,7 +21,10 @@
     rows = images.shape[0]
     piece = rows // PIECES
     sources = (texts, images)
-    onward = (after, before)
+    spot = lax.rem(place, 4) if cycle % 4 == 0 else -1
+    detour = spot == 2
+    onward = (after, jnp.where(detour, after, before))
+    slots = (TEXT, jnp.where(detour, RELAY, IMAGE))
 
     def peer(k):
         return lax.rem(group + k, group_width)
@@ -51,10 +54,26 @@
 
     def far_copy(kind, c):
         return pltpu.make_async_remote_copy(
-            src_ref=sources[kind].at[pl.ds(c * piece, piece)], dst_ref=own_piece(kind, c),
-            send_sem=far_send.at[kind, c], recv_sem=far_recv.at[kind, c],
+            src_ref=sources[kind].at[pl.ds(c * piece, piece)],
+            dst_ref=own_piece(slots[kind], c),
+            send_sem=far_send.at[kind, c], recv_sem=far_recv.at[slots[kind], c],
             device_id=(group, onward[kind]), device_id_type=pl.DeviceIdType.MESH,
         )
+
+    def relay_copy(c):
+        return pltpu.make_async_remote_copy(
+            src_ref=own_piece(RELAY, c), dst_ref=own_piece(IMAGE, c),
+            send_sem=far_send.at[RELAY, c], recv_sem=far_recv.at[IMAGE, c],
+            device_id=(group, lax.rem(place + cycle - 2, cycle)),
+            device_id_type=pl.DeviceIdType.MESH,
+        )
+
+    def far_wait(slot, c):
+        pltpu.make_async_remote_copy(
+            src_ref=own_piece(slot, c), dst_ref=own_piece(slot, c),
+            send_sem=far_send.at[slot, c], recv_sem=far_recv.at[slot, c],
+            device_id=(group, before), device_id_type=pl.DeviceIdType.MESH,
+        ).wait_recv()
 
     def pass_copy(kind, c, k):
         return pltpu.make_async_remote_copy(
@@ -77,7 +96,16 @@
         )
 
     over_peers(greet)
-    pl.semaphore_wait(barrier, group_width + 1)
+
+    @pl.when(spot == 1)
+    def _():
+        pl.semaphore_signal(
+            barrier, inc=1, device_id=(group, lax.rem(place + 2, cycle)),
+            device_id_type=pl.DeviceIdType.MESH,
+        )
+
+    relays = (spot == 3) if cycle % 4 == 0 else False
+    pl.semaphore_wait(barrier, group_width + 1 + jnp.where(relays, 1, 0))
 
     for c in range(PIECES):
         for kind in (TEXT, IMAGE):
@@ -125,8 +153,14 @@
             meet(kind, far[kind, c])
 
     for c in range(PIECES):
-        for kind in (TEXT, IMAGE):
-            far_copy(kind, c).wait_recv()
+
+        @pl.when(spot == 3)
+        def _():
+            far_wait(RELAY, c)
+            relay_copy(c).start()
+
+        for kind in (TEXT, IMAGE):
+            far_wait(kind, c)
             over_peers(lambda k: pass_copy(kind, c, k).start())
         if c > 0:
             meet_far(c - 1)
@@ -136,6 +170,11 @@
     for kind in (TEXT, IMAGE):
         for c in range(PIECES):
             far_copy(kind, c).wait_send()
+
+    @pl.when(spot == 3)
+    def _():
+        for c in range(PIECES):
+            relay_copy(c).wait_send()
 
     def sent(k):
         for kind in (TEXT, IMAGE):
@@ -172,12 +211,12 @@
         out_specs=[pl.BlockSpec(memory_space=pltpu.VMEM)] * 3,
         scratch_shapes=[
             pltpu.VMEM((2, group_width * rows, width), images.dtype),
-            pltpu.VMEM((2, PIECES, group_width * rows // PIECES, width), images.dtype),
+            pltpu.VMEM((3, PIECES, group_width * rows // PIECES, width), images.dtype),
             pltpu.SemaphoreType.DMA((2,)),
             pltpu.SemaphoreType.DMA((2, group_width)),
             pltpu.SemaphoreType.DMA((2, group_width)),
-            pltpu.SemaphoreType.DMA((2, PIECES)),
-            pltpu.SemaphoreType.DMA((2, PIECES)),
+            pltpu.SemaphoreType.DMA((3, PIECES)),
+            pltpu.SemaphoreType.DMA((3, PIECES)),
             pltpu.SemaphoreType.DMA((2, PIECES, group_width)),
             pltpu.SemaphoreType.DMA((2, PIECES, group_width)),
         ],

time: 23.4 us -> 25.4 us (1.085)
  Pallas kernels: 21.3 us -> 23.3 us
    pallas_call x1, Pallas kernels: 20.3 us -> 22.3 us  [shards(): pl.pallas_call(functools.partial(kernel, group_width, cycle), out_shape=s...]
where the time goes in v10:
time: 25.4 us; the launch traced here: 25.2 us
  Pallas kernels  23.3 us (92%)
  between operations  1.93 us (8%)
    pallas_call x1, Pallas kernels, shards(): pl.pallas_call(functools.partial(kernel, group_width, cycle), out_shape=s...  22.3 us
    pallas_call x1, Pallas kernels, shards(): pl.pallas_call(store, out_shape=shapes, in_specs=[pl.BlockSpec(memory_spa...  1.04 us

profile of v10, /device:TPU:3, one launch (start us, length us, event | category | flops | bytes accessed | tf_op | source)
XLA Modules:
  0.0 25.2 jit_solution(10033130794910196955)
XLA Ops:
  1.9 22.3 %shard_map.67 = (f32[128,1152]{1,0:T(8,128)S(1)}, f32[128,1152]{1,0:T(8,128)S(1)}, f32[1,128]{1,0:T(1,128)S(1)}) custom-call(bf16[128,1152]{1,0:T(8,128)(2,1)} %images.1, bf16[128,1152]{1,0:T(8,128)(2,1)} %texts.1, f32[1]{0:T(128)S(6)} %copy.7.scale, f32[1]{0:T(128)S(6)} %copy.8.shift), custom_call_target="tpu_custom_call" | custom-call | flops 603979776 | bytes 2359296 | tf_op jit(solution)/shard_map/pallas_call | solution.py:206
  24.2 1.0 %shard_map.68 = (f32[128,1152]{1,0:T(8,128)}, f32[128,1152]{1,0:T(8,128)}, f32[1,128]{1,0:T(1,128)}) custom-call(f32[128,1152]{1,0:T(8,128)S(1)} %get-tuple-element.9.refs_0_, f32[128,1152]{1,0:T(8,128)S(1)} %get-tuple-element.10.refs_1_, f32[1,128]{1,0:T(1,128)S(1)} %get-tuple-element.11.refs_2_), custom_call_target="tpu_custom_call" | custom-call | bytes 2359296 | tf_op jit(solution)/shard_map/pallas_call | solution.py:235

commit v11 on v3

--- a/solution.py
+++ b/solution.py
@@ -8,7 +8,7 @@
 from jax.sharding import PartitionSpec as P
 
 SPAN = 2
-PIECES = 4
+PIECES = 2
 TEXT, IMAGE = 0, 1
 
 

time: 23.4 us -> 23.4 us (level)
  no operation moved by 1% of the time
where the time goes in v11:
time: 23.4 us; the launch traced here: 23.3 us
  Pallas kernels  21.4 us (91%)
  between operations  1.93 us (8%)
    pallas_call x1, Pallas kernels, shards(): pl.pallas_call(functools.partial(kernel, group_width, cycle), out_shape=s...  20.3 us
    pallas_call x1, Pallas kernels, shards(): pl.pallas_call(store, out_shape=shapes, in_specs=[pl.BlockSpec(memory_spa...  1.04 us

profile of v11, /device:TPU:3, one launch (start us, length us, event | category | flops | bytes accessed | tf_op | source)
XLA Modules:
  0.0 23.3 jit_solution(5775774112044425614)
XLA Ops:
  1.9 20.3 %shard_map.67 = (f32[128,1152]{1,0:T(8,128)S(1)}, f32[128,1152]{1,0:T(8,128)S(1)}, f32[1,128]{1,0:T(1,128)S(1)}) custom-call(bf16[128,1152]{1,0:T(8,128)(2,1)} %images.1, bf16[128,1152]{1,0:T(8,128)(2,1)} %texts.1, f32[1]{0:T(128)S(6)} %copy.7.scale, f32[1]{0:T(128)S(6)} %copy.8.shift), custom_call_target="tpu_custom_call" | custom-call | flops 603979776 | bytes 2359296 | tf_op jit(solution)/shard_map/pallas_call | solution.py:167
  22.2 1.0 %shard_map.68 = (f32[128,1152]{1,0:T(8,128)}, f32[128,1152]{1,0:T(8,128)}, f32[1,128]{1,0:T(1,128)}) custom-call(f32[128,1152]{1,0:T(8,128)S(1)} %get-tuple-element.9.refs_0_, f32[128,1152]{1,0:T(8,128)S(1)} %get-tuple-element.10.refs_1_, f32[1,128]{1,0:T(1,128)S(1)} %get-tuple-element.11.refs_2_), custom_call_target="tpu_custom_call" | custom-call | bytes 2359296 | tf_op jit(solution)/shard_map/pallas_call | solution.py:196
